TPU v7x, 32 devices: a whole 2x2x4 slice. The times are simulated.
32 devices in a mesh: tok: 8 (over z, y), tp: 4 (over x, core).
Axes of the slice: x: 2, y: 2, z: 4, core: 2. Of those that a mesh axis runs over, the one named last changes fastest.
Arguments:
- inputs: bfloat16 [6144, 2304], P('tok'), may hold values from -7 to 7
- seq_lengths: int32 [4], replicated, may hold values from 1024 to 2048, as said below
- gain_attn_in: bfloat16 [2304], P('tok'), may hold values from 0.5 to 1.5
- gain_attn_out: bfloat16 [2304], P('tok'), may hold values from 0.5 to 1.5
- gain_ffn_in: bfloat16 [2304], P('tok'), may hold values from 0.5 to 1.5
- gain_ffn_out: bfloat16 [2304], P('tok'), may hold values from 0.5 to 1.5
- w_query: bfloat16 [2304, 2048], P('tok', 'tp'), may hold values from -2 to 2
- w_key: bfloat16 [2304, 1024], P('tok', 'tp'), may hold values from -2 to 2
- w_value: bfloat16 [2304, 1024], P('tok', 'tp'), may hold values from -0.125 to 0.125
- w_out: bfloat16 [2304, 2048], P('tok', 'tp'), may hold values from -0.125 to 0.125
- w_gate: bfloat16 [2304, 9216], P('tok', 'tp'), may hold values from -0.125 to 0.125
- w_up: bfloat16 [2304, 9216], P('tok', 'tp'), may hold values from -0.125 to 0.125
- w_down: bfloat16 [2304, 9216], P('tok', 'tp'), may hold values from -0.0625 to 0.0625
- out_grad: bfloat16 [6144, 2304], P('tok'), may hold values from -6 to 6
Outputs:
- layer_out: bfloat16 [6144, 2304], P('tok')
- input_grad: float32 [6144, 2304], P('tok')
- gain_attn_in_grad: float32 [2304], P('tok')
- gain_attn_out_grad: float32 [2304], P('tok')
- gain_ffn_in_grad: float32 [2304], P('tok')
- gain_ffn_out_grad: float32 [2304], P('tok')
- w_query_grad: float32 [2304, 2048], P('tok', 'tp')
- w_key_grad: float32 [2304, 1024], P('tok', 'tp')
- w_value_grad: float32 [2304, 1024], P('tok', 'tp')
- w_out_grad: float32 [2304, 2048], P('tok', 'tp')
- w_gate_grad: float32 [2304, 9216], P('tok', 'tp')
- w_up_grad: float32 [2304, 9216], P('tok', 'tp')
- w_down_grad: float32 [2304, 9216], P('tok', 'tp')
Inputs may be any that keep to these rules, and one draw needn't show every extreme that they name: `seq_lengths`: lengths of the 4 packed sequences in order; they sum to 6144, and entries 2k and 2k + 1 sum to 3072.
All inputs are finite; a program needn't handle non-finite values.
Results may differ from a plain program's by a relative error of at most 0.023.
Values may be sent and summed in bfloat16 or wider, within the bound.
A program may use at most 256 MiB of HBM per device.

v0:
```python
from functools import partial
import jax
import jax.numpy as jnp
from jax import lax
from jax.sharding import PartitionSpec as P

HEAD_DIM = 256
REACH = 3
softcap_limit = 50.0
norm_epsilon = 1e-06
rope_base = 10000.0
negative_fill = -1e30


def passed_along(array, axis, by):
    length = lax.axis_size(axis)
    pairs = [(i, i + by) for i in range(length) if 0 <= i + by < length]
    return lax.ppermute(array, axis, pairs)


def norm_apply(values, gain_vec):
    inverse = lax.rsqrt(jnp.mean(values * values, axis=-1, keepdims=True) + norm_epsilon)
    unit_vals = values * inverse
    return (unit_vals * gain_vec, unit_vals, inverse)


def norm_back(gradient, gain_vec, unit_vals, inverse):
    scaled = gradient * gain_vec
    input_part = inverse * (
        scaled - unit_vals * jnp.mean(scaled * unit_vals, axis=-1, keepdims=True)
    )
    return (input_part, jnp.sum(gradient * unit_vals, axis=0))


def token_places(seq_lengths, tok_index):
    starts = jnp.cumsum(seq_lengths) - seq_lengths
    passed = tok_index[:, None] >= starts[None, :]
    segment = jnp.sum(passed.astype(jnp.int32), axis=1) - 1
    seq_start = jnp.max(jnp.where(passed, starts[None, :], 0), axis=1)
    return (segment, tok_index - seq_start)


def rope_tables(position):
    half_dim = HEAD_DIM // 2
    freqs = rope_base ** (-2.0 * jnp.arange(half_dim).astype(jnp.float32) / HEAD_DIM)
    theta = position.astype(jnp.float32)[:, None] * freqs[None, :]
    return (jnp.cos(theta)[:, None, :], jnp.sin(theta)[:, None, :])


def rotate(values, cosine, sine_tab):
    half_dim = values.shape[-1] // 2
    front_half = values[..., :half_dim]
    back_half = values[..., half_dim:]
    return jnp.concatenate(
        [front_half * cosine - back_half * sine_tab, back_half * cosine + front_half * sine_tab],
        axis=-1,
    )


def rotate_back(values, cosine, sine_tab):
    half_dim = values.shape[-1] // 2
    front_half = values[..., :half_dim]
    back_half = values[..., half_dim:]
    return jnp.concatenate(
        [front_half * cosine + back_half * sine_tab, back_half * cosine - front_half * sine_tab],
        axis=-1,
    )


def fetch_window(kv_pair, offset):
    return passed_along((kv_pair[0], kv_pair[1]), "tok", offset)


def return_grads(kv_pair, offset):
    return (
        passed_along(kv_pair[0].astype(jnp.bfloat16), "tok", -offset).astype(jnp.float32),
        passed_along(kv_pair[1].astype(jnp.bfloat16), "tok", -offset).astype(jnp.float32),
    )


def contract_rows(left, right):
    return lax.dot_general(
        left, right, (((0,), (0,)), ((), ())), preferred_element_type=jnp.float32
    )


def contract_cols(left, right):
    return lax.dot_general(
        left, right, (((1,), (1,)), ((), ())), preferred_element_type=jnp.float32
    )


def local(
    inputs,
    seq_lengths,
    gain_attn_in,
    gain_attn_out,
    gain_ffn_in,
    gain_ffn_out,
    w_query,
    w_key,
    w_value,
    w_out,
    w_gate,
    w_up,
    w_down,
    out_grad,
):
    row_count = inputs.shape[0]
    head_cols = w_query.shape[1]
    kv_cols = w_key.shape[1]
    heads_local = head_cols // HEAD_DIM
    kv_local = kv_cols // HEAD_DIM
    group = heads_local // kv_local
    score_scale = HEAD_DIM ** (-0.5)
    tok_place = lax.axis_index("tok")
    own_index = tok_place * row_count + jnp.arange(row_count, dtype=jnp.int32)
    key_index = (tok_place - REACH) * row_count + jnp.arange(
        (REACH + 1) * row_count, dtype=jnp.int32
    )
    seg_query, pos_query = token_places(seq_lengths, own_index)
    seg_key, pos_key = token_places(seq_lengths, key_index)
    allowed = (seg_query[:, None] == seg_key[None, :]) & (pos_key[None, :] <= pos_query[:, None])
    cosine, sine_tab = rope_tables(pos_query)
    attn_mats = (
        lax.all_gather(w_query, "tok", axis=0, tiled=True),
        lax.all_gather(w_key, "tok", axis=0, tiled=True),
        lax.all_gather(w_value, "tok", axis=0, tiled=True),
        lax.all_gather(w_out, "tok", axis=0, tiled=True),
        lax.all_gather(gain_attn_in, "tok", axis=0, tiled=True),
        lax.all_gather(gain_attn_out, "tok", axis=0, tiled=True),
    )
    gain_one = attn_mats[4].astype(jnp.float32)
    gain_two = attn_mats[5].astype(jnp.float32)
    resid = inputs.astype(jnp.float32)
    normed_one, unit_one, inv_one = norm_apply(resid, gain_one)
    hidden_one = normed_one.astype(jnp.bfloat16)
    query_pre = jnp.dot(hidden_one, attn_mats[0], preferred_element_type=jnp.float32)
    key_pre = jnp.dot(hidden_one, attn_mats[1], preferred_element_type=jnp.float32)
    value_vec = jnp.dot(hidden_one, attn_mats[2], preferred_element_type=jnp.float32).astype(
        jnp.bfloat16
    )
    query_rot = rotate(
        query_pre.reshape(row_count, heads_local, HEAD_DIM), cosine, sine_tab
    ).astype(jnp.bfloat16)
    key_rot = (
        rotate(key_pre.reshape(row_count, kv_local, HEAD_DIM), cosine, sine_tab)
        .reshape(row_count, kv_cols)
        .astype(jnp.bfloat16)
    )
    key_parts = [key_rot]
    value_parts = [value_vec]
    for offset in range(1, REACH + 1):
        arrived = fetch_window((key_rot, value_vec), offset)
        key_parts.insert(0, arrived[0])
        value_parts.insert(0, arrived[1])
    key_grp = jnp.concatenate(key_parts, axis=0).reshape(-1, kv_local, HEAD_DIM)
    value_grp = jnp.concatenate(value_parts, axis=0).reshape(-1, kv_local, HEAD_DIM)
    query_grp = query_rot.reshape(row_count, kv_local, group, HEAD_DIM)

    def capped_scores():
        raw_scores = jnp.einsum(
            "qgjd,kgd->gjqk", query_grp, key_grp, preferred_element_type=jnp.float32
        )
        capped = softcap_limit * jnp.tanh(raw_scores * score_scale / softcap_limit)
        return (capped, jnp.where(allowed[None, None], capped, negative_fill))

    capped_fwd, masked_fwd = capped_scores()
    row_max = jnp.max(masked_fwd, axis=-1, keepdims=True)
    exponent = jnp.exp(masked_fwd - row_max)
    row_total = jnp.sum(exponent, axis=-1, keepdims=True)
    log_total = row_max + jnp.log(row_total)
    probs_low = (exponent / row_total).astype(jnp.bfloat16)
    attended = (
        jnp.einsum("gjqk,kgd->qgjd", probs_low, value_grp, preferred_element_type=jnp.float32)
        .reshape(row_count, head_cols)
        .astype(jnp.bfloat16)
    )
    attn_part = contract_cols(attended, attn_mats[3])
    attn_total = lax.psum(attn_part, "tp")
    normed_two, unit_two, inv_two = norm_apply(attn_total, gain_two)
    resid_mid = resid + normed_two
    ffn_mats = (
        lax.all_gather(w_gate, "tok", axis=0, tiled=True),
        lax.all_gather(w_up, "tok", axis=0, tiled=True),
        lax.all_gather(w_down, "tok", axis=0, tiled=True),
        lax.all_gather(gain_ffn_in, "tok", axis=0, tiled=True),
        lax.all_gather(gain_ffn_out, "tok", axis=0, tiled=True),
    )
    gain_three = ffn_mats[3].astype(jnp.float32)
    gain_four = ffn_mats[4].astype(jnp.float32)
    normed_three, unit_three, inv_three = norm_apply(resid_mid, gain_three)
    hidden_two = normed_three.astype(jnp.bfloat16)
    gate_vals = jnp.dot(hidden_two, ffn_mats[0], preferred_element_type=jnp.float32)
    up_vals = jnp.dot(hidden_two, ffn_mats[1], preferred_element_type=jnp.float32)
    gelu_tanh = partial(jax.nn.gelu, approximate=True)
    activated, gelu_pull = jax.vjp(gelu_tanh, gate_vals)
    inner = (activated * up_vals).astype(jnp.bfloat16)
    ffn_part = contract_cols(inner, ffn_mats[2])
    ffn_total = lax.psum(ffn_part, "tp")
    normed_four, unit_four, inv_four = norm_apply(ffn_total, gain_four)
    layer_out = (resid_mid + normed_four).astype(jnp.bfloat16)
    ffn_mats = (
        lax.all_gather(w_gate, "tok", axis=0, tiled=True),
        lax.all_gather(w_up, "tok", axis=0, tiled=True),
        lax.all_gather(w_down, "tok", axis=0, tiled=True),
        lax.all_gather(gain_ffn_in, "tok", axis=0, tiled=True),
        lax.all_gather(gain_ffn_out, "tok", axis=0, tiled=True),
    )
    grad_out = out_grad.astype(jnp.float32)
    d_ffn, grad_four = norm_back(grad_out, gain_four, unit_four, inv_four)
    d_ffn_low = d_ffn.astype(jnp.bfloat16)
    d_inner = jnp.dot(d_ffn_low, ffn_mats[2], preferred_element_type=jnp.float32)
    grad_down = contract_rows(d_ffn_low, inner)
    grad_upvals = (d_inner * activated).astype(jnp.bfloat16)
    grad_gatevals = gelu_pull(d_inner * up_vals)[0].astype(jnp.bfloat16)
    grad_gate = contract_rows(hidden_two, grad_gatevals)
    grad_upmat = contract_rows(hidden_two, grad_upvals)
    d_hidden_part = contract_cols(grad_gatevals, ffn_mats[0]) + contract_cols(
        grad_upvals, ffn_mats[1]
    )
    d_hidden_two = lax.psum(d_hidden_part, "tp")
    mid_add, grad_three = norm_back(d_hidden_two, gain_three, unit_three, inv_three)
    d_mid = grad_out + mid_add
    ffn_sums = (
        lax.psum_scatter(
            grad_gate.astype(jnp.bfloat16), "tok", scatter_dimension=0, tiled=True
        ).astype(jnp.float32),
        lax.psum_scatter(
            grad_upmat.astype(jnp.bfloat16), "tok", scatter_dimension=0, tiled=True
        ).astype(jnp.float32),
        lax.psum_scatter(
            grad_down.astype(jnp.bfloat16), "tok", scatter_dimension=0, tiled=True
        ).astype(jnp.float32),
        lax.psum_scatter(
            grad_three.astype(jnp.bfloat16), "tok", scatter_dimension=0, tiled=True
        ).astype(jnp.float32),
        lax.psum_scatter(
            grad_four.astype(jnp.bfloat16), "tok", scatter_dimension=0, tiled=True
        ).astype(jnp.float32),
    )
    attn_mats = (
        lax.all_gather(w_query, "tok", axis=0, tiled=True),
        lax.all_gather(w_key, "tok", axis=0, tiled=True),
        lax.all_gather(w_value, "tok", axis=0, tiled=True),
        lax.all_gather(w_out, "tok", axis=0, tiled=True),
        lax.all_gather(gain_attn_in, "tok", axis=0, tiled=True),
        lax.all_gather(gain_attn_out, "tok", axis=0, tiled=True),
    )
    d_attn, grad_two = norm_back(d_mid, gain_two, unit_two, inv_two)
    d_attn_low = d_attn.astype(jnp.bfloat16)
    grad_outmat = contract_rows(d_attn_low, attended)
    d_attended = jnp.dot(d_attn_low, attn_mats[3], preferred_element_type=jnp.float32).astype(
        jnp.bfloat16
    )
    d_att_grp = d_attended.reshape(row_count, kv_local, group, HEAD_DIM)
    capped_bwd, masked_bwd = capped_scores()
    probs = jnp.exp(masked_bwd - log_total)
    probs_back = probs.astype(jnp.bfloat16)
    d_probs = jnp.einsum("qgjd,kgd->gjqk", d_att_grp, value_grp, preferred_element_type=jnp.float32)
    d_value_win = jnp.einsum(
        "gjqk,qgjd->kgd", probs_back, d_att_grp, preferred_element_type=jnp.float32
    )
    row_delta = jnp.sum(probs * d_probs, axis=-1, keepdims=True)
    ratio_cap = capped_bwd / softcap_limit
    d_raw = (probs * (d_probs - row_delta) * (1.0 - ratio_cap * ratio_cap) * score_scale).astype(
        jnp.bfloat16
    )
    d_query_rot = jnp.einsum("gjqk,kgd->qgjd", d_raw, key_grp, preferred_element_type=jnp.float32)
    d_key_win = jnp.einsum("gjqk,qgjd->kgd", d_raw, query_grp, preferred_element_type=jnp.float32)
    d_key_slots = d_key_win.reshape(REACH + 1, row_count, kv_cols)
    d_value_slots = d_value_win.reshape(REACH + 1, row_count, kv_cols)
    key_total = d_key_slots[REACH]
    value_total = d_value_slots[REACH]
    for offset in range(1, REACH + 1):
        arrived = return_grads((d_key_slots[REACH - offset], d_value_slots[REACH - offset]), offset)
        key_total = key_total + arrived[0]
        value_total = value_total + arrived[1]
    d_query = (
        rotate_back(d_query_rot.reshape(row_count, heads_local, HEAD_DIM), cosine, sine_tab)
        .reshape(row_count, head_cols)
        .astype(jnp.bfloat16)
    )
    d_key = (
        rotate_back(key_total.reshape(row_count, kv_local, HEAD_DIM), cosine, sine_tab)
        .reshape(row_count, kv_cols)
        .astype(jnp.bfloat16)
    )
    d_value = value_total.astype(jnp.bfloat16)
    grad_query = contract_rows(hidden_one, d_query)
    grad_key = contract_rows(hidden_one, d_key)
    grad_value = contract_rows(hidden_one, d_value)
    d_hidden_one_part = (
        contract_cols(d_query, attn_mats[0])
        + contract_cols(d_key, attn_mats[1])
        + contract_cols(d_value, attn_mats[2])
    )
    d_hidden_one = lax.psum(d_hidden_one_part.astype(jnp.bfloat16), "tp").astype(jnp.float32)
    input_add, grad_one = norm_back(d_hidden_one, gain_one, unit_one, inv_one)
    input_grad = d_mid + input_add
    attn_sums = (
        lax.psum_scatter(
            grad_query.astype(jnp.bfloat16), "tok", scatter_dimension=0, tiled=True
        ).astype(jnp.float32),
        lax.psum_scatter(
            grad_key.astype(jnp.bfloat16), "tok", scatter_dimension=0, tiled=True
        ).astype(jnp.float32),
        lax.psum_scatter(
            grad_value.astype(jnp.bfloat16), "tok", scatter_dimension=0, tiled=True
        ).astype(jnp.float32),
        lax.psum_scatter(
            grad_outmat.astype(jnp.bfloat16), "tok", scatter_dimension=0, tiled=True
        ).astype(jnp.float32),
        lax.psum_scatter(
            grad_one.astype(jnp.bfloat16), "tok", scatter_dimension=0, tiled=True
        ).astype(jnp.float32),
        lax.psum_scatter(
            grad_two.astype(jnp.bfloat16), "tok", scatter_dimension=0, tiled=True
        ).astype(jnp.float32),
    )
    return (
        layer_out,
        input_grad,
        attn_sums[4],
        attn_sums[5],
        ffn_sums[3],
        ffn_sums[4],
        attn_sums[0],
        attn_sums[1],
        attn_sums[2],
        attn_sums[3],
        ffn_sums[0],
        ffn_sums[1],
        ffn_sums[2],
    )


def solution(mesh):
    in_specs = (
        P("tok", None),
        P(),
        P("tok"),
        P("tok"),
        P("tok"),
        P("tok"),
        P("tok", "tp"),
        P("tok", "tp"),
        P("tok", "tp"),
        P("tok", "tp"),
        P("tok", "tp"),
        P("tok", "tp"),
        P("tok", "tp"),
        P("tok", None),
    )
    out_specs = (
        P("tok", None),
        P("tok", None),
        P("tok"),
        P("tok"),
        P("tok"),
        P("tok"),
        P("tok", "tp"),
        P("tok", "tp"),
        P("tok", "tp"),
        P("tok", "tp"),
        P("tok", "tp"),
        P("tok", "tp"),
        P("tok", "tp"),
    )
    return jax.shard_map(local, mesh=mesh, in_specs=in_specs, out_specs=out_specs, check_vma=False)
```

profile of v0, /device:TPU:0, one launch (start us, length us, event | category | flops | bytes accessed | tf_op | source)
XLA Modules:
  0.0 2218.1 jit_solution(15859377549336782163)
XLA Ops:
  23.4 39.7 %all-reduce.9 = (bf16[2304]{0:T(1024)(128)(2,1)}, bf16[2304]{0:T(1024)(128)(2,1)}, bf16[2304]{0:T(1024)(128)(2,1)}, bf16[2304]{0:T(1024)(128)(2,1)}) all-reduce(bf16[2304]{0:T(1024)(128)(2,1)} %dynamic-update-slice, bf16[2304]{0:T(1024)(128)(2,1)} %copy-done.40, ...), channel_id=1, replica_groups=mesh['tok'=8,'tp'=4] {'tok'}, use_global_device_ids=true, to_apply=%add | all-reduce | flops 9216 | bytes 36864
  80.0 17.7 all-gather.10.cloned.1.call-done
  113.1 49.7 %all-gather.12.cloned.1.call-done = bf16[2304,512]{1,0:T(8,128)(2,1)} async-done(((bf16[288,512]{1,0:T(8,128)(2,1)}), bf16[2304,512]{1,0:T(8,128)(2,1)}) %all-gather.12.cloned.1.call-update) | async-done | bytes 2359312 | tf_op jit(solution)/shard_map/all_gather | solution.py:126
  204.6 24.7 %all-gather.14.cloned.1.call-done = bf16[2304,512]{1,0:T(8,128)(2,1)} async-done(((bf16[288,512]{1,0:T(8,128)(2,1)}), bf16[2304,512]{1,0:T(8,128)(2,1)}) %all-gather.14.cloned.1.call-update) | async-done | bytes 2359312 | tf_op jit(solution)/shard_map/all_gather | solution.py:129
  240.4 126.9 %all-reduce.15.cloned.1.call-done = f32[768,2304]{1,0:T(8,128)} async-done(((f32[768,2304]{1,0:T(8,128)}), f32[768,2304]{1,0:T(8,128)}) %all-reduce.15.cloned.1.call-update) | async-done | bytes 7077904 | tf_op jit(solution)/shard_map/psum | solution.py:180
  378.4 143.6 %all-gather.16.cloned.1.call-done = bf16[2304,2304]{1,0:T(8,128)(2,1)} async-done(((bf16[288,2304]{1,0:T(8,128)(2,1)}), bf16[2304,2304]{1,0:T(8,128)(2,1)}) %all-gather.16.cloned.1.call-update) | async-done | bytes 10616848 | tf_op jit(solution)/shard_map/all_gather | solution.py:184
  535.8 139.1 %all-gather.18.cloned.1.call-done = bf16[2304,2304]{1,0:T(8,128)(2,1)} async-done(((bf16[288,2304]{1,0:T(8,128)(2,1)}), bf16[2304,2304]{1,0:T(8,128)(2,1)}) %all-gather.18.cloned.1.call-update) | async-done | bytes 10616848 | tf_op jit(solution)/shard_map/all_gather | solution.py:185
  674.9 15.6 multiply_convert_fusion.2
  690.5 137.2 %all-gather.20.cloned.1.call-done = bf16[2304,2304]{1,0:T(8,128)(2,1)} async-done(((bf16[288,2304]{1,0:T(8,128)(2,1)}), bf16[2304,2304]{1,0:T(8,128)(2,1)}) %all-gather.20.cloned.1.call-update) | async-done | bytes 10616848 | tf_op jit(solution)/shard_map/all_gather | solution.py:186
  844.2 129.2 %all-reduce.17.cloned.1.call-done = f32[768,2304]{1,0:T(8,128)} async-done(((f32[768,2304]{1,0:T(8,128)}), f32[768,2304]{1,0:T(8,128)}) %all-reduce.17.cloned.1.call-update) | async-done | bytes 7077904 | tf_op jit(solution)/shard_map/psum | solution.py:200
  986.7 20.0 multiply_convert_fusion.1
  1006.7 15.1 fusion.115
  1021.8 16.0 convolution_add_fusion
  1039.2 131.4 %all-reduce.19.cloned.1.call-done = f32[768,2304]{1,0:T(8,128)} async-done(((f32[768,2304]{1,0:T(8,128)}), f32[768,2304]{1,0:T(8,128)}) %all-reduce.19.cloned.1.call-update) | async-done | bytes 7077904 | tf_op jit(solution)/shard_map/psum | solution.py:222
  1210.8 17.6 fusion.2
  1228.4 15.2 fusion.1
  1359.3 21.9 all-reduce.21.cloned.1.call-done
  1385.9 38.7 %all-reduce.8 = (bf16[2304]{0:T(1024)(128)(2,1)}, bf16[2304]{0:T(1024)(128)(2,1)}, bf16[2304]{0:T(1024)(128)(2,1)}, bf16[2304]{0:T(1024)(128)(2,1)}) all-reduce(bf16[2304]{0:T(1024)(128)(2,1)} %get-tuple-element.19, bf16[2304]{0:T(1024)(128)(2,1)} %get-tuple-element.15, ...), channel_id=2, replica_groups=mesh['tok'=8,'tp'=4] {'tok'}, use_global_device_ids=true, to_apply=%region_21.22.clone | all-reduce | flops 9216 | bytes 36864
  1450.4 65.4 %reduce-scatter.10.cloned.1.call-done = bf16[288,256]{1,0:T(8,128)(2,1)} async-done(((bf16[2304,256]{1,0:T(8,128)(2,1)}), bf16[288,256]{1,0:T(8,128)(2,1)}) %reduce-scatter.10.cloned.1.call-update) | async-done | bytes 147472 | tf_op jit(solution)/shard_map/reduce_scatter | solution.py:305
  1517.4 70.4 %reduce-scatter.14.cloned.1.call-done = bf16[288,512]{1,0:T(8,128)(2,1)} async-done(((bf16[2304,512]{1,0:T(8,128)(2,1)}), bf16[288,512]{1,0:T(8,128)(2,1)}) %reduce-scatter.14.cloned.1.call-update) | async-done | bytes 294928 | tf_op jit(solution)/shard_map/reduce_scatter | solution.py:311
  1589.7 70.1 %reduce-scatter.8.cloned.1.call-done = bf16[288,512]{1,0:T(8,128)(2,1)} async-done(((bf16[2304,512]{1,0:T(8,128)(2,1)}), bf16[288,512]{1,0:T(8,128)(2,1)}) %reduce-scatter.8.cloned.1.call-update) | async-done | bytes 294928 | tf_op jit(solution)/shard_map/reduce_scatter | solution.py:302
  1661.6 180.7 %reduce-scatter.18.cloned.1.call-done = bf16[288,2304]{1,0:T(8,128)(2,1)} async-done(((bf16[2304,2304]{1,0:T(8,128)(2,1)}), bf16[288,2304]{1,0:T(8,128)(2,1)}) %reduce-scatter.18.cloned.1.call-update) | async-done | bytes 1327120 | tf_op jit(solution)/shard_map/reduce_scatter | solution.py:229
  1845.3 180.0 %reduce-scatter.16.cloned.1.call-done = bf16[288,2304]{1,0:T(8,128)(2,1)} async-done(((bf16[2304,2304]{1,0:T(8,128)(2,1)}), bf16[288,2304]{1,0:T(8,128)(2,1)}) %reduce-scatter.16.cloned.1.call-update) | async-done | bytes 1327120 | tf_op jit(solution)/shard_map/reduce_scatter | solution.py:226
  2028.3 179.5 %reduce-scatter.20.cloned.1.call-done = bf16[288,2304]{1,0:T(8,128)(2,1)} async-done(((bf16[2304,2304]{1,0:T(8,128)(2,1)}), bf16[288,2304]{1,0:T(8,128)(2,1)}) %reduce-scatter.20.cloned.1.call-update) | async-done | bytes 1327120 | tf_op jit(solution)/shard_map/reduce_scatter | solution.py:232
  (262 shorter events, 355.7 us)
Async XLA Ops:
  7.9 89.8 %all-gather.10.cloned.1.call-start = ((), (), s32[]{:S(2)}) async-start(), calls=%async_computation.8 | async-start | bytes 1327104 | tf_op jit(solution)/shard_map/all_gather | solution.py:127
  8.7 154.2 %all-gather.12.cloned.1.call-start = ((), (), s32[]{:S(2)}) async-start(), calls=%async_computation.9 | async-start | bytes 2654208 | tf_op jit(solution)/shard_map/all_gather | solution.py:126
  9.4 219.9 %all-gather.14.cloned.1.call-start = ((), (), s32[]{:S(2)}) async-start(), calls=%async_computation.10 | async-start | bytes 2654208 | tf_op jit(solution)/shard_map/all_gather | solution.py:129
  10.0 357.3 %all-reduce.15.cloned.1.call-start = ((), (), s32[]{:S(2)}) async-start(), calls=%async_computation.11 | async-start | bytes 14155776 | tf_op jit(solution)/shard_map/psum | solution.py:180
  75.8 117.1 %collective-permute-start.2 = (bf16[768,256]{1,0:T(8,128)(2,1)}, bf16[768,256]{1,0:T(8,128)(2,1)}, u32[]{:S(2)}, u32[]{:S(2)}) collective-permute-start(bf16[768,256]{1,0:T(8,128)(2,1)} %convolution_convert_fusion.8), channel_id=1, source_target_pairs={{0,4},{4,8},{8,12},{12,16},{16,20},{20,24},{24,28},{1,5},{5,9},{9,... | collective-permute-start | bytes 1179656 | tf_op jit(solution)/shard_map/ppermute | solution.py:18
  77.9 115.0 %collective-permute-start.1 = (bf16[768,256]{1,0:T(8,128)(2,1)}, bf16[768,256]{1,0:T(8,128)(2,1)}, u32[]{:S(2)}, u32[]{:S(2)}) collective-permute-start(bf16[768,256]{1,0:T(8,128)(2,1)} %convolution_convert_fusion.8), channel_id=1, source_target_pairs={{0,8},{4,12},{8,16},{12,20},{16,24},{20,28},{1,9},{5,13},{9,17},{1... | collective-permute-start | bytes 1179656 | tf_op jit(solution)/shard_map/ppermute | solution.py:18
  102.8 65.9 %collective-permute-start.5 = (bf16[768,256]{0,1:T(8,128)(2,1)}, bf16[768,256]{0,1:T(8,128)(2,1)}, u32[]{:S(2)}, u32[]{:S(2)}) collective-permute-start(bf16[768,256]{0,1:T(8,128)(2,1)} %maximum_bitcast_fusion.6), channel_id=1, source_target_pairs={{0,4},{4,8},{8,12},{12,16},{16,20},{20,24},{24,28},{1,5},{5,9},{9,... | collective-permute-start | bytes 1179656 | tf_op jit(solution)/shard_map/ppermute | solution.py:18
  105.7 72.3 %collective-permute-start.4 = (bf16[768,256]{0,1:T(8,128)(2,1)}, bf16[768,256]{0,1:T(8,128)(2,1)}, u32[]{:S(2)}, u32[]{:S(2)}) collective-permute-start(bf16[768,256]{0,1:T(8,128)(2,1)} %maximum_bitcast_fusion.6), channel_id=1, source_target_pairs={{0,8},{4,12},{8,16},{12,20},{16,24},{20,28},{1,9},{5,13},{9,17},{1... | collective-permute-start | bytes 1179656 | tf_op jit(solution)/shard_map/ppermute | solution.py:18
  110.1 68.0 %collective-permute-start.3 = (bf16[768,256]{0,1:T(8,128)(2,1)}, bf16[768,256]{0,1:T(8,128)(2,1)}, u32[]{:S(2)}, u32[]{:S(2)}) collective-permute-start(bf16[768,256]{0,1:T(8,128)(2,1)} %maximum_bitcast_fusion.6), channel_id=1, source_target_pairs={{0,12},{4,16},{8,20},{12,24},{16,28},{1,13},{5,17},{9,21},{13,25},... | collective-permute-start | bytes 1179656 | tf_op jit(solution)/shard_map/ppermute | solution.py:18
  236.3 285.8 %all-gather.16.cloned.1.call-start = ((), (), s32[]{:S(2)}) async-start(), calls=%async_computation.12 | async-start | bytes 11943936 | tf_op jit(solution)/shard_map/all_gather | solution.py:184
  236.9 438.1 %all-gather.18.cloned.1.call-start = ((), (), s32[]{:S(2)}) async-start(), calls=%async_computation.13 | async-start | bytes 11943936 | tf_op jit(solution)/shard_map/all_gather | solution.py:185
  237.6 590.2 %all-gather.20.cloned.1.call-start = ((), (), s32[]{:S(2)}) async-start(), calls=%async_computation.14 | async-start | bytes 11943936 | tf_op jit(solution)/shard_map/all_gather | solution.py:186
  238.4 735.1 %all-reduce.17.cloned.1.call-start = ((), (), s32[]{:S(2)}) async-start(), calls=%async_computation.15 | async-start | bytes 14155776 | tf_op jit(solution)/shard_map/psum | solution.py:200
  842.7 327.9 %all-reduce.19.cloned.1.call-start = ((), (), s32[]{:S(2)}) async-start(), calls=%async_computation.16 | async-start | bytes 14155776 | tf_op jit(solution)/shard_map/psum | solution.py:222
  1037.8 343.3 %all-reduce.21.cloned.1.call-start = ((), (), s32[]{:S(2)}) async-start(), calls=%async_computation.17 | async-start | bytes 7077888 | tf_op jit(solution)/shard_map/psum | solution.py:298
  1208.2 76.9 %collective-permute-start.9 = (bf16[768,256]{0,1:T(8,128)(2,1)}, bf16[768,256]{0,1:T(8,128)(2,1)S(1)}, u32[]{:S(2)}, u32[]{:S(2)}) collective-permute-start(bf16[768,256]{0,1:T(8,128)(2,1)} %get-tuple-element.46), channel_id=1, source_target_pairs={{4,0},{8,4},{12,8},{16,12},{20,16},{24,20},{28,24},{5,1},{9,5},{13... | collective-permute-start | bytes 1179656 | tf_op jit(solution)/shard_map/ppermute | solution.py:18
  1209.5 75.7 %collective-permute-start.11 = (bf16[768,256]{0,1:T(8,128)(2,1)}, bf16[768,256]{0,1:T(8,128)(2,1)}, u32[]{:S(2)}, u32[]{:S(2)}) collective-permute-start(bf16[768,256]{0,1:T(8,128)(2,1)} %get-tuple-element.47), channel_id=1, source_target_pairs={{12,0},{16,4},{20,8},{24,12},{28,16},{13,1},{17,5},{21,9},{25,13},... | collective-permute-start | bytes 1179656 | tf_op jit(solution)/shard_map/ppermute | solution.py:18
  1299.1 149.7 %reduce-scatter.12.cloned.1.call-start = ((), (), s32[]{:S(2)}) async-start(), calls=%async_computation.20 | async-start | bytes 1327104 | tf_op jit(solution)/shard_map/reduce_scatter | solution.py:308
  1302.7 213.1 %reduce-scatter.10.cloned.1.call-start = ((), (), s32[]{:S(2)}) async-start(), calls=%async_computation.19 | async-start | bytes 1327104 | tf_op jit(solution)/shard_map/reduce_scatter | solution.py:305
  1306.2 281.6 %reduce-scatter.14.cloned.1.call-start = ((), (), s32[]{:S(2)}) async-start(), calls=%async_computation.21 | async-start | bytes 2654208 | tf_op jit(solution)/shard_map/reduce_scatter | solution.py:311
  1312.0 347.8 %reduce-scatter.8.cloned.1.call-start = ((), (), s32[]{:S(2)}) async-start(), calls=%async_computation.18 | async-start | bytes 2654208 | tf_op jit(solution)/shard_map/reduce_scatter | solution.py:302
  1317.1 525.2 %reduce-scatter.18.cloned.1.call-start = ((), (), s32[]{:S(2)}) async-start(), calls=%async_computation.23 | async-start | bytes 11943936 | tf_op jit(solution)/shard_map/reduce_scatter | solution.py:229
  1330.9 694.3 %reduce-scatter.16.cloned.1.call-start = ((), (), s32[]{:S(2)}) async-start(), calls=%async_computation.22 | async-start | bytes 11943936 | tf_op jit(solution)/shard_map/reduce_scatter | solution.py:226
  1344.7 863.2 %reduce-scatter.20.cloned.1.call-start = ((), (), s32[]{:S(2)}) async-start(), calls=%async_computation.24 | async-start | bytes 11943936 | tf_op jit(solution)/shard_map/reduce_scatter | solution.py:232
  (58 other events, 1397.7 us)
Sparse Core Ops, SparseCore 0:
  10.2 43.9 all-gather.7
  56.4 41.2 all-gather.9
  99.9 62.8 all-gather.11
  164.9 64.4 all-gather.13
  236.4 130.8 all-reduce.14
  369.3 152.6 all-gather.15
  524.2 150.6 all-gather.17
  677.1 150.6 all-gather.19
  842.8 130.5 all-reduce.16
  1038.0 132.5 all-reduce.18
  1299.3 81.8 all-reduce.20
  1384.4 64.3 reduce-scatter.11
  1452.8 62.9 reduce-scatter.9
  1519.7 68.0 reduce-scatter.13
  1591.8 67.9 reduce-scatter.7
  1663.2 179.0 reduce-scatter.17
  1846.2 179.0 reduce-scatter.15
  2028.7 179.0 reduce-scatter.19
where the time goes:
time: 2230 us; the launch traced here: 2220 us
  waiting for transfers between devices  1710 us (77%)
  matrix products  240 us (11%)
  other arithmetic  123 us (6%)
  blocking collectives  78.4 us (4%)
  starting transfers between devices  32.9 us (1%)
    reduce_scatter x1, waiting for transfers between devices, local(): lax.psum_scatter(grad_upmat.astype(jnp.bfloat16), 'tok', scatter_dimensio...  181 us
    reduce_scatter x1, waiting for transfers between devices, local(): lax.psum_scatter(grad_gate.astype(jnp.bfloat16), 'tok', scatter_dimension...  180 us
    reduce_scatter x1, waiting for transfers between devices, local(): lax.psum_scatter(grad_down.astype(jnp.bfloat16), 'tok', scatter_dimension...  180 us
    all_gather x1, waiting for transfers between devices, local(): lax.all_gather(w_gate, 'tok', axis=0, tiled=True)  144 us
    all_gather x1, waiting for transfers between devices, local(): lax.all_gather(w_up, 'tok', axis=0, tiled=True)  139 us
    all_gather x1, waiting for transfers between devices, local(): lax.all_gather(w_down, 'tok', axis=0, tiled=True)  137 us
    psum x1, waiting for transfers between devices, local(): d_hidden_two = lax.psum(d_hidden_part, 'tp')  131 us
    psum x1, waiting for transfers between devices, local(): ffn_total = lax.psum(ffn_part, 'tp')  129 us
  transfers between devices with their start and end apart: 30, of which 21 were waited for; matrix products, arithmetic and copies ran while one was open for 11% of the time, Pallas kernels for 0%

commit v1 on v0

--- a/solution.py
+++ b/solution.py
@@ -177,7 +177,7 @@
         .astype(jnp.bfloat16)
     )
     attn_part = contract_cols(attended, attn_mats[3])
-    attn_total = lax.psum(attn_part, "tp")
+    attn_total = jnp.sum(lax.all_gather(attn_part, "tp"), axis=0)
     normed_two, unit_two, inv_two = norm_apply(attn_total, gain_two)
     resid_mid = resid + normed_two
     ffn_mats = (

time: 2230 us -> 2270 us (1.018)
  waiting for transfers between devices: 1710 us -> 1740 us
    all_gather x0 -> x1, waiting for transfers between devices: none -> 168 us  [local(): attn_total = jnp.sum(lax.all_gather(attn_part, 'tp'), axis=0)]
    psum x1 -> x0, waiting for transfers between devices: 127 us -> none  [local(): attn_total = lax.psum(attn_part, 'tp')]
where the time goes in v1:
time: 2270 us; the launch traced here: 2260 us
  waiting for transfers between devices  1740 us (77%)
  matrix products  240 us (11%)
  other arithmetic  136 us (6%)
  blocking collectives  78.4 us (3%)
  starting transfers between devices  33.3 us (1%)
    reduce_scatter x1, waiting for transfers between devices, local(): lax.psum_scatter(grad_upmat.astype(jnp.bfloat16), 'tok', scatter_dimensio...  181 us
    reduce_scatter x1, waiting for transfers between devices, local(): lax.psum_scatter(grad_gate.astype(jnp.bfloat16), 'tok', scatter_dimension...  180 us
    reduce_scatter x1, waiting for transfers between devices, local(): lax.psum_scatter(grad_down.astype(jnp.bfloat16), 'tok', scatter_dimension...  180 us
    all_gather x1, waiting for transfers between devices, local(): attn_total = jnp.sum(lax.all_gather(attn_part, 'tp'), axis=0)  168 us
    all_gather x1, waiting for transfers between devices, local(): lax.all_gather(w_up, 'tok', axis=0, tiled=True)  139 us
    all_gather x1, waiting for transfers between devices, local(): lax.all_gather(w_down, 'tok', axis=0, tiled=True)  137 us
    psum x1, waiting for transfers between devices, local(): d_hidden_two = lax.psum(d_hidden_part, 'tp')  131 us
    all_gather x1, waiting for transfers between devices, local(): lax.all_gather(w_gate, 'tok', axis=0, tiled=True)  129 us
  transfers between devices with their start and end apart: 30, of which 21 were waited for; matrix products, arithmetic and copies ran while one was open for 11% of the time, Pallas kernels for 0%

profile of v1, /device:TPU:0, one launch (start us, length us, event | category | flops | bytes accessed | tf_op | source)
XLA Modules:
  0.0 2257.8 jit_solution(14844756217184954062)
XLA Ops:
  23.4 39.7 %all-reduce.9 = (bf16[2304]{0:T(1024)(128)(2,1)}, bf16[2304]{0:T(1024)(128)(2,1)}, bf16[2304]{0:T(1024)(128)(2,1)}, bf16[2304]{0:T(1024)(128)(2,1)}) all-reduce(bf16[2304]{0:T(1024)(128)(2,1)} %dynamic-update-slice, bf16[2304]{0:T(1024)(128)(2,1)} %copy-done.40, ...), channel_id=1, replica_groups=mesh['tok'=8,'tp'=4] {'tok'}, use_global_device_ids=true, to_apply=%add | all-reduce | flops 9216 | bytes 36864
  80.0 17.8 all-gather.12.cloned.1.call-done
  113.1 49.7 %all-gather.14.cloned.1.call-done = bf16[2304,512]{1,0:T(8,128)(2,1)} async-done(((bf16[288,512]{1,0:T(8,128)(2,1)}), bf16[2304,512]{1,0:T(8,128)(2,1)}) %all-gather.14.cloned.1.call-update) | async-done | bytes 2359312 | tf_op jit(solution)/shard_map/all_gather | solution.py:126
  204.6 24.7 %all-gather.16.cloned.1.call-done = bf16[2304,512]{1,0:T(8,128)(2,1)} async-done(((bf16[288,512]{1,0:T(8,128)(2,1)}), bf16[2304,512]{1,0:T(8,128)(2,1)}) %all-gather.16.cloned.1.call-update) | async-done | bytes 2359312 | tf_op jit(solution)/shard_map/all_gather | solution.py:129
  239.0 168.1 %all-gather.24.cloned.1.call-done = f32[3072,2304]{1,0:T(8,128)} async-done(((f32[768,2304]{1,0:T(8,128)}), f32[3072,2304]{1,0:T(8,128)}) %all-gather.24.cloned.1.call-update) | async-done | bytes 28311568 | tf_op jit(solution)/shard_map/all_gather | solution.py:180
  432.4 129.3 %all-gather.18.cloned.1.call-done = bf16[2304,2304]{1,0:T(8,128)(2,1)} async-done(((bf16[288,2304]{1,0:T(8,128)(2,1)}), bf16[2304,2304]{1,0:T(8,128)(2,1)}) %all-gather.18.cloned.1.call-update) | async-done | bytes 10616848 | tf_op jit(solution)/shard_map/all_gather | solution.py:184
  575.5 139.1 %all-gather.20.cloned.1.call-done = bf16[2304,2304]{1,0:T(8,128)(2,1)} async-done(((bf16[288,2304]{1,0:T(8,128)(2,1)}), bf16[2304,2304]{1,0:T(8,128)(2,1)}) %all-gather.20.cloned.1.call-update) | async-done | bytes 10616848 | tf_op jit(solution)/shard_map/all_gather | solution.py:185
  714.5 15.6 multiply_convert_fusion.2
  730.1 137.3 %all-gather.22.cloned.1.call-done = bf16[2304,2304]{1,0:T(8,128)(2,1)} async-done(((bf16[288,2304]{1,0:T(8,128)(2,1)}), bf16[2304,2304]{1,0:T(8,128)(2,1)}) %all-gather.22.cloned.1.call-update) | async-done | bytes 10616848 | tf_op jit(solution)/shard_map/all_gather | solution.py:186
  884.0 129.2 %all-reduce.14.cloned.1.call-done = f32[768,2304]{1,0:T(8,128)} async-done(((f32[768,2304]{1,0:T(8,128)}), f32[768,2304]{1,0:T(8,128)}) %all-reduce.14.cloned.1.call-update) | async-done | bytes 7077904 | tf_op jit(solution)/shard_map/psum | solution.py:200
  1026.5 20.0 multiply_convert_fusion.1
  1046.5 15.2 fusion.115
  1061.7 16.0 convolution_add_fusion
  1079.1 131.4 %all-reduce.16.cloned.1.call-done = f32[768,2304]{1,0:T(8,128)} async-done(((f32[768,2304]{1,0:T(8,128)}), f32[768,2304]{1,0:T(8,128)}) %all-reduce.16.cloned.1.call-update) | async-done | bytes 7077904 | tf_op jit(solution)/shard_map/psum | solution.py:222
  1250.9 17.4 fusion.2
  1268.3 15.3 fusion.1
  1399.2 21.9 all-reduce.18.cloned.1.call-done
  1425.8 38.7 %all-reduce.8 = (bf16[2304]{0:T(1024)(128)(2,1)}, bf16[2304]{0:T(1024)(128)(2,1)}, bf16[2304]{0:T(1024)(128)(2,1)}, bf16[2304]{0:T(1024)(128)(2,1)}) all-reduce(bf16[2304]{0:T(1024)(128)(2,1)} %get-tuple-element.19, bf16[2304]{0:T(1024)(128)(2,1)} %get-tuple-element.15, ...), channel_id=3, replica_groups=mesh['tok'=8,'tp'=4] {'tok'}, use_global_device_ids=true, to_apply=%region_21.22.clone | all-reduce | flops 9216 | bytes 36864
  1490.4 65.3 %reduce-scatter.10.cloned.1.call-done = bf16[288,256]{1,0:T(8,128)(2,1)} async-done(((bf16[2304,256]{1,0:T(8,128)(2,1)}), bf16[288,256]{1,0:T(8,128)(2,1)}) %reduce-scatter.10.cloned.1.call-update) | async-done | bytes 147472 | tf_op jit(solution)/shard_map/reduce_scatter | solution.py:305
  1557.3 70.4 %reduce-scatter.14.cloned.1.call-done = bf16[288,512]{1,0:T(8,128)(2,1)} async-done(((bf16[2304,512]{1,0:T(8,128)(2,1)}), bf16[288,512]{1,0:T(8,128)(2,1)}) %reduce-scatter.14.cloned.1.call-update) | async-done | bytes 294928 | tf_op jit(solution)/shard_map/reduce_scatter | solution.py:311
  1629.6 70.3 %reduce-scatter.8.cloned.1.call-done = bf16[288,512]{1,0:T(8,128)(2,1)} async-done(((bf16[2304,512]{1,0:T(8,128)(2,1)}), bf16[288,512]{1,0:T(8,128)(2,1)}) %reduce-scatter.8.cloned.1.call-update) | async-done | bytes 294928 | tf_op jit(solution)/shard_map/reduce_scatter | solution.py:302
  1701.8 180.7 %reduce-scatter.18.cloned.1.call-done = bf16[288,2304]{1,0:T(8,128)(2,1)} async-done(((bf16[2304,2304]{1,0:T(8,128)(2,1)}), bf16[288,2304]{1,0:T(8,128)(2,1)}) %reduce-scatter.18.cloned.1.call-update) | async-done | bytes 1327120 | tf_op jit(solution)/shard_map/reduce_scatter | solution.py:229
  1885.4 179.8 %reduce-scatter.16.cloned.1.call-done = bf16[288,2304]{1,0:T(8,128)(2,1)} async-done(((bf16[2304,2304]{1,0:T(8,128)(2,1)}), bf16[288,2304]{1,0:T(8,128)(2,1)}) %reduce-scatter.16.cloned.1.call-update) | async-done | bytes 1327120 | tf_op jit(solution)/shard_map/reduce_scatter | solution.py:226
  2068.2 179.5 %reduce-scatter.20.cloned.1.call-done = bf16[288,2304]{1,0:T(8,128)(2,1)} async-done(((bf16[2304,2304]{1,0:T(8,128)(2,1)}), bf16[288,2304]{1,0:T(8,128)(2,1)}) %reduce-scatter.20.cloned.1.call-update) | async-done | bytes 1327120 | tf_op jit(solution)/shard_map/reduce_scatter | solution.py:232
  (267 shorter events, 368.9 us)
Async XLA Ops:
  7.9 89.8 %all-gather.12.cloned.1.call-start = ((), (), s32[]{:S(2)}) async-start(), calls=%async_computation.8 | async-start | bytes 1327104 | tf_op jit(solution)/shard_map/all_gather | solution.py:127
  8.7 154.1 %all-gather.14.cloned.1.call-start = ((), (), s32[]{:S(2)}) async-start(), calls=%async_computation.9 | async-start | bytes 2654208 | tf_op jit(solution)/shard_map/all_gather | solution.py:126
  9.4 219.9 %all-gather.16.cloned.1.call-start = ((), (), s32[]{:S(2)}) async-start(), calls=%async_computation.10 | async-start | bytes 2654208 | tf_op jit(solution)/shard_map/all_gather | solution.py:129
  10.0 397.2 %all-gather.24.cloned.1.call-start = ((), (), s32[]{:S(2)}) async-start(), calls=%async_computation.24 | async-start | bytes 35389440 | tf_op jit(solution)/shard_map/all_gather | solution.py:180
  75.8 117.3 %collective-permute-start.2 = (bf16[768,256]{1,0:T(8,128)(2,1)}, bf16[768,256]{1,0:T(8,128)(2,1)}, u32[]{:S(2)}, u32[]{:S(2)}) collective-permute-start(bf16[768,256]{1,0:T(8,128)(2,1)} %convolution_convert_fusion.8), channel_id=1, source_target_pairs={{0,4},{4,8},{8,12},{12,16},{16,20},{20,24},{24,28},{1,5},{5,9},{9,... | collective-permute-start | bytes 1179656 | tf_op jit(solution)/shard_map/ppermute | solution.py:18
  77.9 115.3 %collective-permute-start.1 = (bf16[768,256]{1,0:T(8,128)(2,1)}, bf16[768,256]{1,0:T(8,128)(2,1)}, u32[]{:S(2)}, u32[]{:S(2)}) collective-permute-start(bf16[768,256]{1,0:T(8,128)(2,1)} %convolution_convert_fusion.8), channel_id=1, source_target_pairs={{0,8},{4,12},{8,16},{12,20},{16,24},{20,28},{1,9},{5,13},{9,17},{1... | collective-permute-start | bytes 1179656 | tf_op jit(solution)/shard_map/ppermute | solution.py:18
  102.8 65.9 %collective-permute-start.5 = (bf16[768,256]{0,1:T(8,128)(2,1)}, bf16[768,256]{0,1:T(8,128)(2,1)}, u32[]{:S(2)}, u32[]{:S(2)}) collective-permute-start(bf16[768,256]{0,1:T(8,128)(2,1)} %maximum_bitcast_fusion.6), channel_id=1, source_target_pairs={{0,4},{4,8},{8,12},{12,16},{16,20},{20,24},{24,28},{1,5},{5,9},{9,... | collective-permute-start | bytes 1179656 | tf_op jit(solution)/shard_map/ppermute | solution.py:18
  105.7 72.6 %collective-permute-start.4 = (bf16[768,256]{0,1:T(8,128)(2,1)}, bf16[768,256]{0,1:T(8,128)(2,1)}, u32[]{:S(2)}, u32[]{:S(2)}) collective-permute-start(bf16[768,256]{0,1:T(8,128)(2,1)} %maximum_bitcast_fusion.6), channel_id=1, source_target_pairs={{0,8},{4,12},{8,16},{12,20},{16,24},{20,28},{1,9},{5,13},{9,17},{1... | collective-permute-start | bytes 1179656 | tf_op jit(solution)/shard_map/ppermute | solution.py:18
  110.1 68.2 %collective-permute-start.3 = (bf16[768,256]{0,1:T(8,128)(2,1)}, bf16[768,256]{0,1:T(8,128)(2,1)}, u32[]{:S(2)}, u32[]{:S(2)}) collective-permute-start(bf16[768,256]{0,1:T(8,128)(2,1)} %maximum_bitcast_fusion.6), channel_id=1, source_target_pairs={{0,12},{4,16},{8,20},{12,24},{16,28},{1,13},{5,17},{9,21},{13,25},... | collective-permute-start | bytes 1179656 | tf_op jit(solution)/shard_map/ppermute | solution.py:18
  236.3 325.4 %all-gather.18.cloned.1.call-start = ((), (), s32[]{:S(2)}) async-start(), calls=%async_computation.11 | async-start | bytes 11943936 | tf_op jit(solution)/shard_map/all_gather | solution.py:184
  236.8 477.7 %all-gather.20.cloned.1.call-start = ((), (), s32[]{:S(2)}) async-start(), calls=%async_computation.12 | async-start | bytes 11943936 | tf_op jit(solution)/shard_map/all_gather | solution.py:185
  237.6 629.8 %all-gather.22.cloned.1.call-start = ((), (), s32[]{:S(2)}) async-start(), calls=%async_computation.13 | async-start | bytes 11943936 | tf_op jit(solution)/shard_map/all_gather | solution.py:186
  238.3 774.9 %all-reduce.14.cloned.1.call-start = ((), (), s32[]{:S(2)}) async-start(), calls=%async_computation.14 | async-start | bytes 14155776 | tf_op jit(solution)/shard_map/psum | solution.py:200
  882.6 327.9 %all-reduce.16.cloned.1.call-start = ((), (), s32[]{:S(2)}) async-start(), calls=%async_computation.15 | async-start | bytes 14155776 | tf_op jit(solution)/shard_map/psum | solution.py:222
  1077.7 343.4 %all-reduce.18.cloned.1.call-start = ((), (), s32[]{:S(2)}) async-start(), calls=%async_computation.16 | async-start | bytes 7077888 | tf_op jit(solution)/shard_map/psum | solution.py:298
  1248.3 76.8 %collective-permute-start.9 = (bf16[768,256]{0,1:T(8,128)(2,1)}, bf16[768,256]{0,1:T(8,128)(2,1)S(1)}, u32[]{:S(2)}, u32[]{:S(2)}) collective-permute-start(bf16[768,256]{0,1:T(8,128)(2,1)} %get-tuple-element.46), channel_id=1, source_target_pairs={{4,0},{8,4},{12,8},{16,12},{20,16},{24,20},{28,24},{5,1},{9,5},{13... | collective-permute-start | bytes 1179656 | tf_op jit(solution)/shard_map/ppermute | solution.py:18
  1249.6 75.5 %collective-permute-start.11 = (bf16[768,256]{0,1:T(8,128)(2,1)}, bf16[768,256]{0,1:T(8,128)(2,1)}, u32[]{:S(2)}, u32[]{:S(2)}) collective-permute-start(bf16[768,256]{0,1:T(8,128)(2,1)} %get-tuple-element.47), channel_id=1, source_target_pairs={{12,0},{16,4},{20,8},{24,12},{28,16},{13,1},{17,5},{21,9},{25,13},... | collective-permute-start | bytes 1179656 | tf_op jit(solution)/shard_map/ppermute | solution.py:18
  1339.1 149.7 %reduce-scatter.12.cloned.1.call-start = ((), (), s32[]{:S(2)}) async-start(), calls=%async_computation.19 | async-start | bytes 1327104 | tf_op jit(solution)/shard_map/reduce_scatter | solution.py:308
  1342.6 213.1 %reduce-scatter.10.cloned.1.call-start = ((), (), s32[]{:S(2)}) async-start(), calls=%async_computation.18 | async-start | bytes 1327104 | tf_op jit(solution)/shard_map/reduce_scatter | solution.py:305
  1346.1 281.6 %reduce-scatter.14.cloned.1.call-start = ((), (), s32[]{:S(2)}) async-start(), calls=%async_computation.20 | async-start | bytes 2654208 | tf_op jit(solution)/shard_map/reduce_scatter | solution.py:311
  1351.9 348.1 %reduce-scatter.8.cloned.1.call-start = ((), (), s32[]{:S(2)}) async-start(), calls=%async_computation.17 | async-start | bytes 2654208 | tf_op jit(solution)/shard_map/reduce_scatter | solution.py:302
  1357.2 525.2 %reduce-scatter.18.cloned.1.call-start = ((), (), s32[]{:S(2)}) async-start(), calls=%async_computation.22 | async-start | bytes 11943936 | tf_op jit(solution)/shard_map/reduce_scatter | solution.py:229
  1371.0 694.3 %reduce-scatter.16.cloned.1.call-start = ((), (), s32[]{:S(2)}) async-start(), calls=%async_computation.21 | async-start | bytes 11943936 | tf_op jit(solution)/shard_map/reduce_scatter | solution.py:226
  1384.7 863.1 %reduce-scatter.20.cloned.1.call-start = ((), (), s32[]{:S(2)}) async-start(), calls=%async_computation.23 | async-start | bytes 11943936 | tf_op jit(solution)/shard_map/reduce_scatter | solution.py:232
  (60 other events, 1270.7 us)
Sparse Core Ops, SparseCore 0:
  10.2 43.9 all-gather.9
  56.4 41.2 all-gather.11
  99.9 62.8 all-gather.13
  164.9 64.3 all-gather.15
  236.4 170.7 all-gather.23
  409.2 152.4 all-gather.17
  563.9 150.6 all-gather.19
  716.7 150.6 all-gather.21
  882.7 130.5 all-reduce.13
  1077.8 132.5 all-reduce.15
  1339.2 81.8 all-reduce.17
  1424.3 64.3 reduce-scatter.11
  1492.7 62.9 reduce-scatter.9
  1559.6 68.0 reduce-scatter.13
  1631.7 68.2 reduce-scatter.7
  1703.4 179.0 reduce-scatter.17
  1886.3 178.8 reduce-scatter.15
  2068.7 179.0 reduce-scatter.19
